TPU v7x, 32 devices: a whole 2x2x4 slice. The times are simulated.
32 devices in a mesh: groups: 2 (over x), tensor: 16 (over z, y, core).
Axes of the slice: x: 2, y: 2, z: 4, core: 2. Of those that a mesh axis runs over, the one named last changes fastest.
Arguments:
- resid: bfloat16 [256, 8192], P(('groups', 'tensor')), parts along dimension 0, may hold values from -100 to 100
- gain: float32 [8192], replicated, may hold values from 0.5 to 1.5
- head: bfloat16 [24000, 8192], P('tensor'), may hold values from -0.176776695 to 0.176776695
- peer: bfloat16 [256, 24000], P('groups', 'tensor'), parts along dimension 0, may hold values from -16 to 260
- labels: int32 [256], P('groups'), parts along dimension 0, may hold values from 0 to 23999
Outputs:
- loss: float32 [2], P('groups'), parts along dimension 0
- input_gradient: bfloat16 [256, 8192], P(('groups', 'tensor')), parts along dimension 0
- head_grad: bfloat16 [48000, 8192], P(('groups', 'tensor')), parts along dimension 0
- gain_gradient: float32 [16384], P('groups'), parts along dimension 0
There are 2 independent parts, one for each index of `groups`. A program takes and returns all parts, laid end to end along the dimension named above; an argument that names none is the same for every part. Nothing has to cross between parts.
All inputs are finite; a program needn't handle non-finite values.
Results may differ from a plain program's by a relative error of at most 0.0055.
Values may be sent and summed in bfloat16 or wider, within the bound.
A program may use at most 128 MiB of HBM per device.

v0:
```python
import jax
import jax.numpy as jnp
from jax import lax
from jax.sharding import PartitionSpec as P

BETA = 0.5
EPS = 1e-05


def per_device(resid, gain, head, peer, labels):
    vocab_dev = head.shape[0]
    offset = lax.axis_index("tensor") * vocab_dev
    widened_rows = resid.astype(jnp.float32)
    inverse_scale = lax.rsqrt(jnp.mean(widened_rows * widened_rows, axis=1, keepdims=True) + EPS)
    scaled_rows = lax.all_gather(
        (widened_rows * inverse_scale * gain).astype(jnp.bfloat16), "tensor", axis=0, tiled=True
    )
    logits = jnp.dot(scaled_rows, head.T, preferred_element_type=jnp.float32)
    other = peer.astype(jnp.float32)
    column = offset + jnp.arange(vocab_dev, dtype=jnp.int32)[None, :]
    match = column == labels[:, None]
    label_part = jnp.sum(jnp.where(match, logits, 0.0), axis=1, keepdims=True)
    top_s, top_p = lax.pmax(
        (jnp.max(logits, axis=1, keepdims=True), jnp.max(other, axis=1, keepdims=True)), "tensor"
    )
    student_exp = jnp.exp(logits - top_s)
    peer_exp = jnp.exp(other - top_p)
    sum_s, sum_p, cross_raw, label_logit = lax.psum(
        (
            jnp.sum(student_exp, axis=1, keepdims=True),
            jnp.sum(peer_exp, axis=1, keepdims=True),
            jnp.sum(peer_exp * (other - logits), axis=1, keepdims=True),
            label_part,
        ),
        "tensor",
    )
    cross = cross_raw / sum_p
    student_lse = top_s + jnp.log(sum_s)
    peer_lse = top_p + jnp.log(sum_p)
    per_token = student_lse - label_logit + BETA * (cross - peer_lse + student_lse)
    loss = jnp.mean(per_token).reshape(1)
    dlogits = (
        (1.0 + BETA) * (student_exp / sum_s) - match.astype(jnp.float32) - BETA * (peer_exp / sum_p)
    ).astype(jnp.bfloat16)
    head_grad = jnp.dot(dlogits.T, scaled_rows, preferred_element_type=jnp.float32).astype(
        jnp.bfloat16
    )
    normalized_grad = lax.psum_scatter(
        jnp.dot(dlogits, head, preferred_element_type=jnp.float32),
        "tensor",
        scatter_dimension=0,
        tiled=True,
    )
    centered_input = widened_rows * inverse_scale
    gain_gradient = lax.psum(jnp.sum(normalized_grad * centered_input, axis=0), "tensor")
    gain_weighted = gain * normalized_grad
    input_gradient = (
        inverse_scale * gain_weighted
        - centered_input
        * inverse_scale
        * jnp.mean(gain_weighted * centered_input, axis=1, keepdims=True)
    ).astype(jnp.bfloat16)
    return (loss, input_gradient, head_grad, gain_gradient)


def solution(mesh):
    return jax.shard_map(
        per_device,
        mesh=mesh,
        in_specs=(
            P(("groups", "tensor"), None),
            P(),
            P("tensor", None),
            P("groups", "tensor"),
            P("groups"),
        ),
        out_specs=(
            P("groups"),
            P(("groups", "tensor"), None),
            P(("groups", "tensor"), None),
            P("groups"),
        ),
        check_vma=False,
    )
```

profile of v0, /device:TPU:0, one launch (start us, length us, event | category | flops | bytes accessed | tf_op | source)
XLA Modules:
  0.0 283.4 jit_solution(5205822451064650779)
XLA Ops:
  7.2 0.0 copy-start.1
  7.2 0.0 copy-start.4
  7.2 0.0 all-gather.2.cloned.1.call-start
  7.2 1.1 fusion.21
  8.4 1.7 fusion.15
  10.0 0.0 all-gather.2.cloned.1.call-update
  10.1 0.0 reduce-scatter.2.cloned.1.call-start
  10.1 1.2 reduce_max.26
  11.3 43.6 %all-gather.2.cloned.1.call-done = bf16[128,8192]{1,0:T(8,128)(2,1)} async-done(((bf16[8,8192]{1,0:T(8,128)(2,1)}), bf16[128,8192]{1,0:T(8,128)(2,1)}) %all-gather.2.cloned.1.call-update) | async-done | bytes 2097168 | tf_op jit(solution)/shard_map/all_gather | solution.py:15
  54.9 12.0 %fusion.25 = (f32[128]{0:T(128)S(1)}, f32[128,1500]{0,1:T(8,128)S(1)}) fusion(bf16[128,8192]{1,0:T(8,128)(2,1)} %all-gather.2.cloned.1.call-done, bf16[1500,8192]{1,0:T(8,128)(2,1)} %param.7), kind=kOutput, calls=%fused_computation.36 | convolution fusion | flops 3145920000 | bytes 27441664 | tf_op jit(solution)/shard_map/dot_general | solution.py:18
  66.9 0.0 copy-start
  66.9 31.6 %all-reduce.2 = (f32[128,1]{0,1:T(1,128)S(1)}, f32[128,1]{0,1:T(1,128)S(1)}) all-reduce(f32[128,1]{0,1:T(1,128)S(1)} %bitcast_convert_fusion, f32[128,1]{0,1:T(1,128)S(1)} %bitcast.31), channel_id=1, replica_groups=mesh['groups'=2,'tensor'=16] {'tensor'}, use_global_device_ids=true, to_apply=%region_8.9 | all-reduce | flops 256 | bytes 2048 | tf_op jit(solution)/shard_map/pmax | solution.py:23
  98.4 0.0 copy-done.1
  98.4 0.0 copy-done.4
  98.4 0.4 fusion.10
  98.8 29.7 %all-reduce.1 = (f32[128,1]{0,1:T(1,128)S(1)}, f32[128,1]{0,1:T(1,128)S(1)}) all-reduce(f32[128,1]{0,1:T(1,128)S(1)} %bitcast.30, f32[128,1]{0,1:T(1,128)S(1)} %bitcast.29), channel_id=1, replica_groups=mesh['groups'=2,'tensor'=16] {'tensor'}, use_global_device_ids=true, to_apply=%region_12.13 | all-reduce | flops 256 | bytes 2048 | tf_op jit(solution)/shard_map/psum | solution.py:28
  128.5 0.0 copy-start.2
  128.5 0.0 copy-start.3
  128.5 14.2 %fusion.23 = f32[128,8192]{1,0:T(8,128)} fusion(bf16[1500,8192]{1,0:T(8,128)(2,1)} %param.7, bf16[128,1500]{0,1:T(8,128)(2,1)S(1)} %copy-done.1, f32[128,1500]{0,1:T(8,128)S(1)} %get-tuple-element.18, f32[128]{0:T(128)S(1)} %bitcast.23, f32[128]{0:T(128)S(1)} %bitcast.25, f32[128]{0:T(128)S(1)} %bitcast.18, s32[128]{0:T(128)S(1)} %copy-done.4, ...), kind=kOutput, calls=%fused_computation.35 | convolution fusion | flops 3148032000 | bytes 29930864 | tf_op jit(solution)/shard_map/dot_general | solution.py:49
  142.7 0.0 reduce-scatter.2.cloned.1.call-update
  142.7 0.0 copy-done
  142.7 12.8 %convolution_convert_fusion = bf16[1500,8192]{1,0:T(8,128)(2,1)} fusion(bf16[128,8192]{1,0:T(8,128)(2,1)S(1)} %copy-done, bf16[128,1500]{0,1:T(8,128)(2,1)S(1)} %copy-done.1, f32[128,1500]{0,1:T(8,128)S(1)} %get-tuple-element.18, f32[128]{0:T(128)S(1)} %bitcast.24, f32[128]{0:T(128)S(1)} %bitcast.26, f32[128]{0:T(128)S(1)} %bitcast.19, s32[128]{0:T(128)S(1)} %copy-done.4, ...), kind=kOutput, calls=%fused_computation | convolution fusion | flops 3160320000 | bytes 27833712 | tf_op jit(solution)/shard_map/dot_general | solution.py:45
  155.5 56.9 %reduce-scatter.2.cloned.1.call-done = f32[8,8192]{1,0:T(8,128)} async-done(((f32[128,8192]{1,0:T(8,128)}), f32[8,8192]{1,0:T(8,128)}) %reduce-scatter.2.cloned.1.call-update) | async-done | bytes 262160 | tf_op jit(solution)/shard_map/reduce_scatter | solution.py:48
  212.5 0.0 copy-done.2
  212.5 0.0 copy-done.3
  212.5 1.3 fusion.20
  213.7 58.7 %all-reduce = (f32[128,1]{0,1:T(1,128)S(1)}, f32[128,1]{0,1:T(1,128)S(1)}, f32[8192]{0:T(1024)}) all-reduce(f32[128,1]{0,1:T(1,128)S(1)} %bitcast.27, f32[128,1]{0,1:T(1,128)S(1)} %bitcast.28, f32[8192]{0:T(1024)S(1)} %get-tuple-element.7), channel_id=1, replica_groups=mesh['groups'=2,'tensor'=16] {'tensor'}, use_global_device_ids=true, to_apply=%region_10.11 | all-reduce | flops 8448 | bytes 67584 | tf_op jit(solution)/shard_map/psum | solution.py:28
  272.5 0.6 add_reduce_fusion
  273.7 1.7 fusion.18
  (4 shorter events, 0.0 us)
Async XLA Ops:
  7.2 91.3 %copy-start.1 = (bf16[128,1500]{0,1:T(8,128)(2,1)S(1)}, bf16[128,1500]{0,1:T(8,128)(2,1)}, u32[]{:S(2)}) copy-start(bf16[128,1500]{0,1:T(8,128)(2,1)} %param.8) | copy-start | bytes 1152004
  7.2 91.3 %copy-start.4 = (s32[128]{0:T(128)S(1)}, s32[128]{0:T(128)}, u32[]{:S(2)}) copy-start(s32[128]{0:T(128)} %param.9) | copy-start | bytes 1540
  7.2 47.7 %all-gather.2.cloned.1.call-start = ((), (), s32[]{:S(2)}) async-start(), calls=%async_computation.1 | async-start | bytes 2228224 | tf_op jit(solution)/shard_map/all_gather | solution.py:15
  10.1 202.4 %reduce-scatter.2.cloned.1.call-start = ((), (), s32[]{:S(2)}) async-start(), calls=%async_computation.2 | async-start | bytes 4456448 | tf_op jit(solution)/shard_map/reduce_scatter | solution.py:48
  66.9 75.8 %copy-start = (bf16[128,8192]{1,0:T(8,128)(2,1)S(1)}, bf16[128,8192]{1,0:T(8,128)(2,1)}, u32[]{:S(2)}) copy-start(bf16[128,8192]{1,0:T(8,128)(2,1)} %all-gather.2.cloned.1.call-done) | copy-start | bytes 6291460
  128.5 83.9 %copy-start.2 = (bf16[8,8192]{1,0:T(8,128)(2,1)S(1)}, bf16[8,8192]{1,0:T(8,128)(2,1)}, u32[]{:S(2)}) copy-start(bf16[8,8192]{1,0:T(8,128)(2,1)} %param.5) | copy-start | bytes 393220
  128.5 83.9 %copy-start.3 = (f32[8192]{0:T(1024)S(1)}, f32[8192]{0:T(1024)}, u32[]{:S(2)}) copy-start(f32[8192]{0:T(1024)} %param.6) | copy-start | bytes 98308
Sparse Core Ops, SparseCore 0:
  10.8 44.0 all-gather.1
  142.8 69.5 reduce-scatter.1
where the time goes:
time: 284 us; the launch traced here: 283 us
  blocking collectives  120 us (42%)
  waiting for transfers between devices  101 us (36%)
  matrix products  38.9 us (14%)
  between operations  15.9 us (6%)
  other arithmetic  8.04 us (3%)
    psum x2, blocking collectives, per_device(): lax.psum((jnp.sum(student_exp, axis=1, keepdims=True), jnp.sum(peer_exp,...  88.4 us
    reduce_scatter x1, waiting for transfers between devices, per_device(): lax.psum_scatter(jnp.dot(dlogits, head, preferred_element_type=jnp.float3...  56.9 us
    all_gather x1, waiting for transfers between devices, per_device(): lax.all_gather((widened_rows * inverse_scale * gain).astype(jnp.bfloat16)...  43.6 us
    pmax x1, blocking collectives, per_device(): lax.pmax((jnp.max(logits, axis=1, keepdims=True), jnp.max(other, axis=1,...  31.6 us
    dot_general x1, matrix products, per_device(): jnp.dot(dlogits, head, preferred_element_type=jnp.float32)  14.2 us
    dot_general x1, matrix products, per_device(): jnp.dot(dlogits.T, scaled_rows, preferred_element_type=jnp.float32)  12.8 us
    dot_general x1, matrix products, per_device(): logits = jnp.dot(scaled_rows, head.T, preferred_element_type=jnp.float32)  12 us
  transfers between devices with their start and end apart: 2, of which 2 were waited for; matrix products, arithmetic and copies ran while one was open for 5% of the time, Pallas kernels for 0%

commit v1 on v0

v1 whole, which is shorter than its diff:
```python
import functools

import jax
import jax.numpy as jnp
from jax import lax
from jax.experimental import pallas as pl
from jax.experimental.pallas import tpu as pltpu
from jax.sharding import PartitionSpec as P

BETA = 0.5
EPS = 1e-05
PARTS = 4
CHUNK = 512
VMEM_BYTES = 58 * 1024 * 1024


def remote(src, dst, send, recv, device):
    return pltpu.make_async_remote_copy(
        src_ref=src,
        dst_ref=dst,
        send_sem=send,
        recv_sem=recv,
        device_id={"tensor": device},
        device_id_type=pl.DeviceIdType.MESH,
    )


def head_kernel(
    n,
    resid_ref,
    gain_ref,
    head_ref,
    peer_ref,
    labels_ref,
    loss_ref,
    input_grad_ref,
    gain_grad_ref,
    dlogits_ref,
    normed_out,
    hbuf,
    normed,
    xhat,
    xswap,
    xchip,
    logits,
    other,
    stat,
    dl,
    acc,
    sib_out,
    sib_in,
    y_out,
    y_in,
    z_out,
    z_in,
    own,
    dnfull,
    gparts,
    gfull,
    head_sem,
    swap_sem,
    az_send,
    ay_send,
    ab_send,
    ac_recv,
    ab_recv,
    st_send,
    st_recv,
    sib_sem,
    y_sem,
    z_send,
    z_recv,
    f_send,
    f_recv,
    g_send,
    g_recv,
    h_sem,
    out_sem,
):
    nk, vocab, bk = hbuf.shape
    _, tokens, half = normed.shape
    rows = resid_ref.shape[0]
    pair = 2 * rows
    w = half // PARTS
    sub = w // bk
    nz = n // 4
    chips = n // 2

    me = lax.axis_index("tensor")
    c = me % 2
    y = (me // 2) % 2
    z = me // 4
    chip = z * 2 + y
    sibling = chip * 2 + (1 - c)
    across = (z * 2 + (1 - y)) * 2 + c

    def head_copy(k):
        return pltpu.make_async_copy(
            head_ref.at[:, pl.ds(k * bk, bk)], hbuf.at[k], head_sem.at[k]
        )

    barrier = pltpu.get_barrier_semaphore()

    def greet(d, carry):
        pl.semaphore_signal(
            barrier, inc=1, device_id={"tensor": (me + d) % n}, device_id_type=pl.DeviceIdType.MESH
        )
        return carry

    lax.fori_loop(1, n, greet, 0)

    for p in range(PARTS):
        for h in range(2):
            for s in range(sub):
                head_copy(h * (nk // 2) + p * sub + s).start()

    wide = resid_ref[...].astype(jnp.float32)
    scale = lax.rsqrt(jnp.mean(wide * wide, axis=1, keepdims=True) + EPS)
    for h in range(2):
        xhat[h] = wide[:, h * half : (h + 1) * half] * scale

    pl.semaphore_wait(barrier, n - 1)

    swap = remote(xhat.at[1 - c], xswap, swap_sem.at[0], swap_sem.at[1], sibling)
    swap.start()
    swap.wait()
    mine = xhat[c]
    theirs = xswap[...]
    first = c == 0
    xchip[pl.ds(0, rows), :] = jnp.where(first, mine, theirs)
    xchip[pl.ds(rows, rows), :] = jnp.where(first, theirs, mine)
    normed[c, pl.ds(pl.multiple_of(chip * pair, 16), pair), :] = (
        xchip[...] * gain_ref[c]
    ).astype(jnp.bfloat16)

    def block(chip_i, p):
        return normed.at[c, pl.ds(pl.multiple_of(chip_i * pair, 16), pair), pl.ds(p * w, w)]

    def block_b(chip_i, p):
        return normed.at[1 - c, pl.ds(pl.multiple_of(chip_i * pair, 16), pair), pl.ds(p * w, w)]

    def along(d):
        return (z + d) % nz

    def to_z(p, d):
        b = block(chip, p)
        return remote(
            b, b, az_send.at[p, d], ac_recv.at[p, chip], (along(d) * 2 + y) * 2 + c
        )

    def to_y(p, d):
        j = along(d) * 2 + y
        b = block(j, p)
        return remote(b, b, ay_send.at[p, d], ac_recv.at[p, j], across)

    def to_sibling(p, j):
        b = block(j, p)
        return remote(b, b, ab_send.at[p, j], ab_recv.at[p, j], sibling)

    def arrived(p, j):
        b = block(j, p)
        remote(b, b, ay_send.at[p, 0], ac_recv.at[p, j], across).wait_recv()

    def arrived_b(p, j):
        b = block_b(j, p)
        remote(b, b, ab_send.at[p, j], ab_recv.at[p, j], sibling).wait_recv()

    for p in range(PARTS):
        to_y(p, 0).start()
        for d in range(1, nz):
            to_z(p, d).start()
        to_sibling(p, chip).start()

    other[...] = jnp.transpose(peer_ref[...].astype(jnp.float32))
    ptop = jnp.max(other[...], axis=0, keepdims=True)
    psum = jnp.sum(jnp.exp(other[...] - ptop), axis=0, keepdims=True)
    stat[me, 2:3, :] = ptop
    stat[me, 3:4, :] = psum
    logits[...] = jnp.zeros_like(logits)

    def add_logits(p):
        def step(i, carry):
            h = i // sub
            at = p * sub + i % sub
            k = h * (nk // 2) + at
            x = normed[h, :, pl.ds(pl.multiple_of(at * bk, bk), bk)]
            logits[...] += lax.dot_general(
                hbuf[k], x, (((1,), (1,)), ((), ())), preferred_element_type=jnp.float32
            )
            return carry

        lax.fori_loop(0, 2 * sub, step, 0)

    for i in range(PARTS + 2):
        if i < PARTS:
            for d in range(1, nz):
                j = along(d) * 2 + y
                arrived(i, j)
                to_y(i, d).start()
                to_sibling(i, j).start()
        if 0 <= i - 1 < PARTS:
            for d in range(nz):
                j = along(d) * 2 + (1 - y)
                arrived(i - 1, j)
                to_sibling(i - 1, j).start()
        if 0 <= i - 2 < PARTS:
            p = i - 2
            for j in range(chips):
                arrived_b(p, j)
            for h in range(2):
                for s in range(sub):
                    head_copy(h * (nk // 2) + p * sub + s).wait()
            add_logits(p)

    out_normed = pltpu.make_async_copy(normed, normed_out, out_sem.at[0])
    out_normed.start()

    column = me * vocab + lax.broadcasted_iota(jnp.int32, (vocab, tokens), 0)
    match = column == labels_ref[...]
    top = jnp.max(logits[...], axis=0, keepdims=True)
    stat[me, 0:1, :] = top
    stat[me, 1:2, :] = jnp.sum(jnp.exp(logits[...] - top), axis=0, keepdims=True)
    stat[me, 4:5, :] = jnp.sum(
        jnp.exp(other[...] - ptop) * (other[...] - logits[...]), axis=0, keepdims=True
    )
    stat[me, 5:6, :] = jnp.sum(jnp.where(match, logits[...], 0.0), axis=0, keepdims=True)
    stat[me, 6:8, :] = jnp.zeros((2, tokens), jnp.float32)

    def stat_copy(d):
        return remote(
            stat.at[me], stat.at[me], st_send.at[d], st_recv.at[me], (me + d) % n
        )

    def send_stat(d, carry):
        stat_copy(d).start()
        return carry

    def wait_stat(d, carry):
        j = (me + d) % n
        remote(stat.at[j], stat.at[j], st_send.at[d], st_recv.at[j], j).wait_recv()
        return carry

    lax.fori_loop(1, n, send_stat, 0)
    lax.fori_loop(1, n, wait_stat, 0)

    top_all = stat[0, 0:1, :]
    ptop_all = stat[0, 2:3, :]
    for j in range(1, n):
        top_all = jnp.maximum(top_all, stat[j, 0:1, :])
        ptop_all = jnp.maximum(ptop_all, stat[j, 2:3, :])
    sum_s = jnp.zeros_like(top_all)
    sum_p = jnp.zeros_like(top_all)
    cross = jnp.zeros_like(top_all)
    label_logit = jnp.zeros_like(top_all)
    for j in range(n):
        sum_s += stat[j, 1:2, :] * jnp.exp(stat[j, 0:1, :] - top_all)
        weight = jnp.exp(stat[j, 2:3, :] - ptop_all)
        sum_p += stat[j, 3:4, :] * weight
        cross += stat[j, 4:5, :] * weight
        label_logit += stat[j, 5:6, :]
    student_lse = top_all + jnp.log(sum_s)
    peer_lse = ptop_all + jnp.log(sum_p)
    per_token = student_lse - label_logit + BETA * (cross / sum_p - peer_lse + student_lse)
    loss_ref[...] = jnp.mean(per_token, axis=1, keepdims=True)

    grad = (
        (1.0 + BETA) / sum_s * jnp.exp(logits[...] - top_all)
        - match.astype(jnp.float32)
        - BETA / sum_p * jnp.exp(other[...] - ptop_all)
    )
    dlogits_ref[...] = grad.astype(jnp.bfloat16)
    dl[...] = jnp.transpose(grad).astype(jnp.bfloat16)

    def product(h, at):
        return jnp.dot(dl[...], hbuf[h * (nk // 2) + at], preferred_element_type=jnp.float32)

    def sib_copy(p):
        return remote(sib_out.at[p], sib_in.at[p], sib_sem.at[0, p], sib_sem.at[1, p], sibling)

    def y_copy(p):
        return remote(y_out.at[p], y_in.at[p], y_sem.at[0, p], y_sem.at[1, p], across)

    def z_copy(p, d):
        return remote(
            z_out.at[p, d],
            z_in.at[p, d],
            z_send.at[p, d],
            z_recv.at[p, d],
            (along(d) * 2 + y) * 2 + c,
        )

    def f_copy(p):
        return remote(
            own.at[p, pl.ds(pl.multiple_of((1 - c) * rows, 8), rows), :],
            dnfull.at[c, :, pl.ds(p * w, w)],
            f_send.at[p],
            f_recv.at[p],
            sibling,
        )

    def f_arrival(p):
        return remote(
            dnfull.at[1 - c, :, pl.ds(p * w, w)],
            dnfull.at[1 - c, :, pl.ds(p * w, w)],
            f_send.at[p],
            f_recv.at[p],
            sibling,
        )

    for i in range(PARTS + 3):
        if i < PARTS:

            def other_half(s, carry, i=i):
                sib_out[i, :, pl.ds(pl.multiple_of(s * bk, bk), bk)] = product(
                    1 - c, i * sub + s
                ).astype(jnp.bfloat16)
                return carry

            def own_half(s, carry, i=i):
                acc[i, :, pl.ds(pl.multiple_of(s * bk, bk), bk)] = product(c, i * sub + s)
                return carry

            lax.fori_loop(0, sub, other_half, 0)
            sib_copy(i).start()
            lax.fori_loop(0, sub, own_half, 0)
        if 0 <= i - 1 < PARTS:
            p = i - 1
            sib_copy(p).wait_recv()
            for d in range(nz):
                at = pl.ds(pl.multiple_of((d * 2 + 1 - y) * pair, 16), pair)
                y_out[p, d] = (acc[p, at, :] + sib_in[p, at, :].astype(jnp.float32)).astype(
                    jnp.bfloat16
                )
            y_copy(p).start()
        if 0 <= i - 2 < PARTS:
            p = i - 2
            y_copy(p).wait_recv()
            for d in range(nz):
                to = along(d)
                at = pl.ds(pl.multiple_of((to * 2 + y) * pair, 16), pair)
                total = (
                    acc[p, at, :]
                    + sib_in[p, at, :].astype(jnp.float32)
                    + y_in[p, to].astype(jnp.float32)
                )
                if d == 0:
                    own[p] = total
                else:
                    z_out[p, d] = total.astype(jnp.bfloat16)
                    z_copy(p, d).start()
        if 0 <= i - 3 < PARTS:
            p = i - 3
            total = own[p]
            for d in range(1, nz):
                z_copy(p, d).wait_recv()
                total += z_in[p, d].astype(jnp.float32)
            own[p] = total
            f_copy(p).start()
            dnfull[c, :, pl.ds(p * w, w)] = own[p, pl.ds(pl.multiple_of(c * rows, 8), rows), :]
            gparts[chip, :, pl.ds(p * w, w)] = jnp.sum(
                total * xchip[:, pl.ds(p * w, w)], axis=0, keepdims=True
            )

    def g_copy(d):
        to = (chip + d) % chips
        return remote(
            gparts.at[chip], gparts.at[chip], g_send.at[d], g_recv.at[chip], to * 2 + c
        )

    def send_g(d, carry):
        g_copy(d).start()
        return carry

    def wait_g(d, carry):
        j = (chip + d) % chips
        remote(gparts.at[j], gparts.at[j], g_send.at[d], g_recv.at[j], sibling).wait_recv()
        return carry

    lax.fori_loop(1, chips, send_g, 0)

    for p in range(PARTS):
        f_arrival(p).wait_recv()
    mean = jnp.zeros((rows, 1), jnp.float32)
    for h in range(2):
        mean += jnp.sum(gain_ref[h] * dnfull[h] * xhat[h], axis=1, keepdims=True)
    mean = mean / (2 * half)
    for h in range(2):
        input_grad_ref[:, h * half : (h + 1) * half] = (
            scale * (gain_ref[h] * dnfull[h]) - xhat[h] * scale * mean
        ).astype(jnp.bfloat16)

    lax.fori_loop(1, chips, wait_g, 0)
    total = gparts[0]
    for j in range(1, chips):
        total += gparts[j]
    gfull[c] = total
    last = remote(gfull.at[c], gfull.at[c], h_sem.at[0], h_sem.at[1], sibling)
    last.start()
    last.wait_send()
    remote(gfull.at[1 - c], gfull.at[1 - c], h_sem.at[0], h_sem.at[1], sibling).wait_recv()
    gain_grad_ref[...] = gfull[...]

    for p in range(PARTS):
        for d in range(nz):
            to_y(p, d).wait_send()
            if d:
                to_z(p, d).wait_send()
                z_copy(p, d).wait_send()
        for j in range(chips):
            to_sibling(p, j).wait_send()
        sib_copy(p).wait_send()
        y_copy(p).wait_send()
        f_copy(p).wait_send()

    def drain_stat(d, carry):
        stat_copy(d).wait_send()
        return carry

    def drain_g(d, carry):
        g_copy(d).wait_send()
        return carry

    lax.fori_loop(1, n, drain_stat, 0)
    lax.fori_loop(1, chips, drain_g, 0)
    out_normed.wait()


def head_grad_kernel(dlogits_ref, normed_ref, out_ref):
    out_ref[...] = jnp.dot(
        dlogits_ref[...], normed_ref[...], preferred_element_type=jnp.float32
    ).astype(jnp.bfloat16)


def per_device(n, resid, gain, head, peer, labels):
    rows, depth = resid.shape
    tokens, vocab = peer.shape
    half = depth // 2
    w = half // PARTS
    bk = min(CHUNK, w)
    nk = depth // bk
    nz = n // 4
    chips = n // 2
    pair = 2 * rows
    f32, bf16 = jnp.float32, jnp.bfloat16
    dma = pltpu.SemaphoreType.DMA
    vmem = pl.BlockSpec(memory_space=pltpu.VMEM)
    hbm = pl.BlockSpec(memory_space=pl.ANY)
    loss, input_grad, gain_grad, dlogits, normed = pl.pallas_call(
        functools.partial(head_kernel, n),
        out_shape=(
            jax.ShapeDtypeStruct((1, 1), f32),
            jax.ShapeDtypeStruct((rows, depth), bf16),
            jax.ShapeDtypeStruct((2, 1, half), f32),
            jax.ShapeDtypeStruct((vocab, tokens), bf16),
            jax.ShapeDtypeStruct((2, tokens, half), bf16),
        ),
        in_specs=[vmem, vmem, hbm, vmem, vmem],
        out_specs=(vmem, vmem, vmem, vmem, hbm),
        scratch_shapes=[
            pltpu.VMEM((nk, vocab, bk), bf16),
            pltpu.VMEM((2, tokens, half), bf16),
            pltpu.VMEM((2, rows, half), f32),
            pltpu.VMEM((rows, half), f32),
            pltpu.VMEM((pair, half), f32),
            pltpu.VMEM((vocab, tokens), f32),
            pltpu.VMEM((vocab, tokens), f32),
            pltpu.VMEM((n, 8, tokens), f32),
            pltpu.VMEM((tokens, vocab), bf16),
            pltpu.VMEM((PARTS, tokens, w), f32),
            pltpu.VMEM((PARTS, tokens, w), bf16),
            pltpu.VMEM((PARTS, tokens, w), bf16),
            pltpu.VMEM((PARTS, nz, pair, w), bf16),
            pltpu.VMEM((PARTS, nz, pair, w), bf16),
            pltpu.VMEM((PARTS, nz, pair, w), bf16),
            pltpu.VMEM((PARTS, nz, pair, w), bf16),
            pltpu.VMEM((PARTS, pair, w), f32),
            pltpu.VMEM((2, rows, half), f32),
            pltpu.VMEM((chips, 1, half), f32),
            pltpu.VMEM((2, 1, half), f32),
            dma((nk,)),
            dma((2,)),
            dma((PARTS, nz)),
            dma((PARTS, nz)),
            dma((PARTS, chips)),
            dma((PARTS, chips)),
            dma((PARTS, chips)),
            dma((n,)),
            dma((n,)),
            dma((2, PARTS)),
            dma((2, PARTS)),
            dma((PARTS, nz)),
            dma((PARTS, nz)),
            dma((PARTS,)),
            dma((PARTS,)),
            dma((chips,)),
            dma((chips,)),
            dma((2,)),
            dma((1,)),
        ],
        compiler_params=pltpu.CompilerParams(
            collective_id=0, has_side_effects=True, vmem_limit_bytes=VMEM_BYTES
        ),
        cost_estimate=pl.CostEstimate(
            flops=4 * tokens * vocab * depth,
            bytes_accessed=2 * vocab * depth,
            transcendentals=4 * tokens * vocab,
        ),
    )(resid, gain.reshape(2, 1, half), head, peer, labels.reshape(1, tokens))

    per_half = half // bk
    head_grad = pl.pallas_call(
        head_grad_kernel,
        grid=(nk,),
        out_shape=jax.ShapeDtypeStruct((vocab, depth), bf16),
        in_specs=[
            pl.BlockSpec((vocab, tokens), lambda k: (0, 0)),
            pl.BlockSpec((None, tokens, bk), lambda k: (k // per_half, 0, k % per_half)),
        ],
        out_specs=pl.BlockSpec((vocab, bk), lambda k: (0, k)),
        compiler_params=pltpu.CompilerParams(vmem_limit_bytes=VMEM_BYTES),
        cost_estimate=pl.CostEstimate(
            flops=2 * tokens * vocab * depth,
            bytes_accessed=2 * vocab * depth,
            transcendentals=0,
        ),
    )(dlogits, normed)
    return loss.reshape(1), input_grad, head_grad, gain_grad.reshape(depth)


def solution(mesh):
    return jax.shard_map(
        functools.partial(per_device, mesh.shape["tensor"]),
        mesh=mesh,
        in_specs=(
            P(("groups", "tensor"), None),
            P(),
            P("tensor", None),
            P("groups", "tensor"),
            P("groups"),
        ),
        out_specs=(
            P("groups"),
            P(("groups", "tensor"), None),
            P(("groups", "tensor"), None),
            P("groups"),
        ),
        check_vma=False,
    )
```

time: 284 us -> 89.7 us (0.32)
  blocking collectives: 120 us -> 0 us
  waiting for transfers between devices: 101 us -> 0 us
  Pallas kernels: 0 us -> 83.5 us
  matrix products: 38.9 us -> 0 us
  between operations: 15.9 us -> 2.49 us
  other arithmetic: 8.04 us -> 0 us
  local copies, waits for them, and re-layouts: 0.02 us -> 3.2 us
    psum x2 -> x0, blocking collectives: 88.4 us -> none  [per_device(): lax.psum((jnp.sum(student_exp, axis=1, keepdims=True), jnp.sum(peer_exp,...]
    pallas_call x0 -> x2, Pallas kernels: none -> 83.5 us  [the longest x1 67.2 us: per_device(): pl.pallas_call(functools.partial(head_kernel, n), out_shape=(jax.ShapeDty...]
    reduce_scatter x1 -> x0, waiting for transfers between devices: 56.9 us -> none  [per_device(): lax.psum_scatter(jnp.dot(dlogits, head, preferred_element_type=jnp.float3...]
    all_gather x1 -> x0, waiting for transfers between devices: 43.6 us -> none  [per_device(): lax.all_gather((widened_rows * inverse_scale * gain).astype(jnp.bfloat16)...]
    dot_general x3 -> x0, matrix products: 38.9 us -> none  [the longest x1 14.2 us: per_device(): jnp.dot(dlogits, head, preferred_element_type=jnp.float32)]
    pmax x1 -> x0, blocking collectives: 31.6 us -> none  [per_device(): lax.pmax((jnp.max(logits, axis=1, keepdims=True), jnp.max(other, axis=1,...]
    reduce_sum x4 -> x0, other arithmetic: 3.41 us -> none  [the longest x1 1.27 us: per_device(): jnp.sum(normalized_grad * centered_input, axis=0)]
    convert_element_type x2 -> x0, other arithmetic: 3.4 us -> none  [the longest x1 1.73 us: per_device(): input_gradient = (inverse_scale * gain_weighted - centered_input * invers...]
  transfers between devices with their start and end apart: 2 -> 0, of which waited for: 2 -> 0; matrix products, arithmetic and copies ran while one was open for 5% -> 0% of each run, Pallas kernels for 0% -> 0%
where the time goes in v1:
time: 89.7 us; the launch traced here: 89.2 us
  Pallas kernels  83.5 us (93%)
  local copies, waits for them, and re-layouts  3.2 us (4%)
  between operations  2.49 us (3%)
    pallas_call x1, Pallas kernels, per_device(): pl.pallas_call(functools.partial(head_kernel, n), out_shape=(jax.ShapeDty...  67.2 us
    pallas_call x1, Pallas kernels, per_device(): pl.pallas_call(head_grad_kernel, grid=(nk,), out_shape=jax.ShapeDtypeStru...  16.3 us
    unnamed x7, local copies, waits for them, and re-layouts  3.2 us

profile of v1, /device:TPU:0, one launch (start us, length us, event | category | flops | bytes accessed | tf_op | source)
XLA Modules:
  0.0 89.2 jit_solution(3988387535040049856)
XLA Ops:
  0.6 1.9 %copy.9.peer_ref = bf16[128,1500]{1,0:T(8,128)(2,1)} copy(bf16[128,1500]{0,1:T(8,128)(2,1)} %param.8) | data formatting | bytes 768000 | tf_op args[3]
  2.5 67.2 %shard_map.84 = (f32[1,1]{1,0:T(1,128)}, bf16[8,8192]{1,0:T(8,128)(2,1)}, f32[2,1,4096]{2,1,0:T(1,128)}, bf16[1500,128]{1,0:T(8,128)(2,1)}, bf16[2,128,4096]{2,1,0:T(8,128)(2,1)}) custom-call(bf16[8,8192]{1,0:T(8,128)(2,1)} %resid_ref.1, f32[2,1,4096]{2,1,0:T(1,128)} %bitcast.4, bf16[1500,8192]{1,0:T(8,128)(2,1)} %head_ref.1, ...), custom_call_target="tpu_custom_call" | custom-call | flops 6291456000 | bytes 24576000 | tf_op jit(solution)/shard_map/pallas_call | solution.py:448
  69.7 0.0 copy-start
  69.7 0.0 copy-start.1
  69.7 16.3 %shard_map.85 = bf16[1500,8192]{1,0:T(8,128)(2,1)} custom-call(bf16[1500,128]{1,0:T(8,128)(2,1)} %get-tuple-element.11.dlogits_ref, bf16[2,128,4096]{2,1,0:T(8,128)(2,1)} %get-tuple-element.12.normed_ref), custom_call_target="tpu_custom_call" | custom-call | flops 3145728000 | bytes 24576000 | tf_op jit(solution)/shard_map/pallas_call | solution.py:511
  86.7 0.0 copy-done
  86.8 0.7 copy.14
  87.4 0.0 copy-done.1
  87.4 0.6 copy.15
Async XLA Ops:
  69.7 17.0 %copy-start = (bf16[8,8192]{1,0:T(8,128)(2,1)S(1)}, bf16[8,8192]{1,0:T(8,128)(2,1)}, u32[]{:S(2)}) copy-start(bf16[8,8192]{1,0:T(8,128)(2,1)} %get-tuple-element.19) | copy-start | bytes 393220
  69.7 17.7 %copy-start.1 = (f32[2,1,4096]{2,1,0:T(1,128)S(1)}, f32[2,1,4096]{2,1,0:T(1,128)}, u32[]{:S(2)}) copy-start(f32[2,1,4096]{2,1,0:T(1,128)} %get-tuple-element.13) | copy-start | bytes 98308

commit v2 on v1

--- a/solution.py
+++ b/solution.py
@@ -11,6 +11,8 @@
 EPS = 1e-05
 PARTS = 4
 CHUNK = 512
+GROUPED = 1
+OUT_COLUMNS = 1024
 VMEM_BYTES = 58 * 1024 * 1024
 
 
@@ -44,6 +46,8 @@
     xchip,
     logits,
     other,
+    student_exp,
+    peer_exp,
     stat,
     dl,
     acc,
@@ -171,9 +175,10 @@
             to_z(p, d).start()
         to_sibling(p, chip).start()
 
-    other[...] = jnp.transpose(peer_ref[...].astype(jnp.float32))
+    other[...] = peer_ref[...].astype(jnp.float32)
     ptop = jnp.max(other[...], axis=0, keepdims=True)
-    psum = jnp.sum(jnp.exp(other[...] - ptop), axis=0, keepdims=True)
+    peer_exp[...] = jnp.exp(other[...] - ptop)
+    psum = jnp.sum(peer_exp[...], axis=0, keepdims=True)
     stat[me, 2:3, :] = ptop
     stat[me, 3:4, :] = psum
     logits[...] = jnp.zeros_like(logits)
@@ -219,9 +224,10 @@
     match = column == labels_ref[...]
     top = jnp.max(logits[...], axis=0, keepdims=True)
     stat[me, 0:1, :] = top
-    stat[me, 1:2, :] = jnp.sum(jnp.exp(logits[...] - top), axis=0, keepdims=True)
+    student_exp[...] = jnp.exp(logits[...] - top)
+    stat[me, 1:2, :] = jnp.sum(student_exp[...], axis=0, keepdims=True)
     stat[me, 4:5, :] = jnp.sum(
-        jnp.exp(other[...] - ptop) * (other[...] - logits[...]), axis=0, keepdims=True
+        peer_exp[...] * (other[...] - logits[...]), axis=0, keepdims=True
     )
     stat[me, 5:6, :] = jnp.sum(jnp.where(match, logits[...], 0.0), axis=0, keepdims=True)
     stat[me, 6:8, :] = jnp.zeros((2, tokens), jnp.float32)
@@ -264,9 +270,9 @@
     loss_ref[...] = jnp.mean(per_token, axis=1, keepdims=True)
 
     grad = (
-        (1.0 + BETA) / sum_s * jnp.exp(logits[...] - top_all)
+        (1.0 + BETA) * jnp.exp(top - top_all) / sum_s * student_exp[...]
         - match.astype(jnp.float32)
-        - BETA / sum_p * jnp.exp(other[...] - ptop_all)
+        - BETA * jnp.exp(ptop - ptop_all) / sum_p * peer_exp[...]
     )
     dlogits_ref[...] = grad.astype(jnp.bfloat16)
     dl[...] = jnp.transpose(grad).astype(jnp.bfloat16)
@@ -305,6 +311,18 @@
             f_send.at[p],
             f_recv.at[p],
             sibling,
+        )
+
+    per_group = max(PARTS // GROUPED, 1)
+    groups = PARTS // per_group
+
+    def g_piece(j, q):
+        return gparts.at[j, :, pl.ds(q * per_group * w, per_group * w)]
+
+    def g_copy(q, d):
+        to = (chip + d) % chips
+        return remote(
+            g_piece(chip, q), g_piece(chip, q), g_send.at[q, d], g_recv.at[q, chip], to * 2 + c
         )
 
     for i in range(PARTS + 3):
@@ -360,23 +378,14 @@
             gparts[chip, :, pl.ds(p * w, w)] = jnp.sum(
                 total * xchip[:, pl.ds(p * w, w)], axis=0, keepdims=True
             )
-
-    def g_copy(d):
-        to = (chip + d) % chips
-        return remote(
-            gparts.at[chip], gparts.at[chip], g_send.at[d], g_recv.at[chip], to * 2 + c
-        )
-
-    def send_g(d, carry):
-        g_copy(d).start()
-        return carry
-
-    def wait_g(d, carry):
-        j = (chip + d) % chips
-        remote(gparts.at[j], gparts.at[j], g_send.at[d], g_recv.at[j], sibling).wait_recv()
-        return carry
-
-    lax.fori_loop(1, chips, send_g, 0)
+            if (p + 1) % per_group == 0:
+                q = p // per_group
+
+                def send_g(d, carry, q=q):
+                    g_copy(q, d).start()
+                    return carry
+
+                lax.fori_loop(1, chips, send_g, 0)
 
     for p in range(PARTS):
         f_arrival(p).wait_recv()
@@ -389,7 +398,16 @@
             scale * (gain_ref[h] * dnfull[h]) - xhat[h] * scale * mean
         ).astype(jnp.bfloat16)
 
-    lax.fori_loop(1, chips, wait_g, 0)
+    for q in range(groups):
+
+        def wait_g(d, carry, q=q):
+            j = (chip + d) % chips
+            remote(
+                g_piece(j, q), g_piece(j, q), g_send.at[q, d], g_recv.at[q, j], sibling
+            ).wait_recv()
+            return carry
+
+        lax.fori_loop(1, chips, wait_g, 0)
     total = gparts[0]
     for j in range(1, chips):
         total += gparts[j]
@@ -417,7 +435,8 @@
         return carry
 
     def drain_g(d, carry):
-        g_copy(d).wait_send()
+        for q in range(groups):
+            g_copy(q, d).wait_send()
         return carry
 
     lax.fori_loop(1, n, drain_stat, 0)
@@ -425,7 +444,15 @@
     out_normed.wait()
 
 
-def head_grad_kernel(dlogits_ref, normed_ref, out_ref):
+def head_grad_kernel(
+    dlogits_ref, normed_ref, loss_in, input_in, gain_in, out_ref, loss_ref, input_ref, gain_ref
+):
+    @pl.when(pl.program_id(0) == 0)
+    def _():
+        loss_ref[...] = loss_in[...]
+        input_ref[...] = input_in[...]
+        gain_ref[...] = gain_in[...]
+
     out_ref[...] = jnp.dot(
         dlogits_ref[...], normed_ref[...], preferred_element_type=jnp.float32
     ).astype(jnp.bfloat16)
@@ -462,6 +489,8 @@
             pltpu.VMEM((2, rows, half), f32),
             pltpu.VMEM((rows, half), f32),
             pltpu.VMEM((pair, half), f32),
+            pltpu.VMEM((vocab, tokens), f32),
+            pltpu.VMEM((vocab, tokens), f32),
             pltpu.VMEM((vocab, tokens), f32),
             pltpu.VMEM((vocab, tokens), f32),
             pltpu.VMEM((n, 8, tokens), f32),
@@ -492,8 +521,8 @@
             dma((PARTS, nz)),
             dma((PARTS,)),
             dma((PARTS,)),
-            dma((chips,)),
-            dma((chips,)),
+            dma((PARTS, chips)),
+            dma((PARTS, chips)),
             dma((2,)),
             dma((1,)),
         ],
@@ -505,25 +534,37 @@
             bytes_accessed=2 * vocab * depth,
             transcendentals=4 * tokens * vocab,
         ),
-    )(resid, gain.reshape(2, 1, half), head, peer, labels.reshape(1, tokens))
-
-    per_half = half // bk
-    head_grad = pl.pallas_call(
+    )(resid, gain.reshape(2, 1, half), head, peer.T, labels.reshape(1, tokens))
+
+    wide = min(OUT_COLUMNS, half)
+    per_half = half // wide
+    small = [
+        pl.BlockSpec((1, 1), lambda k: (0, 0)),
+        pl.BlockSpec((rows, depth), lambda k: (0, 0)),
+        pl.BlockSpec((2, 1, half), lambda k: (0, 0, 0)),
+    ]
+    head_grad, loss, input_grad, gain_grad = pl.pallas_call(
         head_grad_kernel,
-        grid=(nk,),
-        out_shape=jax.ShapeDtypeStruct((vocab, depth), bf16),
+        grid=(depth // wide,),
+        out_shape=(
+            jax.ShapeDtypeStruct((vocab, depth), bf16),
+            jax.ShapeDtypeStruct((1, 1), f32),
+            jax.ShapeDtypeStruct((rows, depth), bf16),
+            jax.ShapeDtypeStruct((2, 1, half), f32),
+        ),
         in_specs=[
             pl.BlockSpec((vocab, tokens), lambda k: (0, 0)),
-            pl.BlockSpec((None, tokens, bk), lambda k: (k // per_half, 0, k % per_half)),
-        ],
-        out_specs=pl.BlockSpec((vocab, bk), lambda k: (0, k)),
+            pl.BlockSpec((None, tokens, wide), lambda k: (k // per_half, 0, k % per_half)),
+        ]
+        + small,
+        out_specs=[pl.BlockSpec((vocab, wide), lambda k: (0, k))] + small,
         compiler_params=pltpu.CompilerParams(vmem_limit_bytes=VMEM_BYTES),
         cost_estimate=pl.CostEstimate(
             flops=2 * tokens * vocab * depth,
             bytes_accessed=2 * vocab * depth,
             transcendentals=0,
         ),
-    )(dlogits, normed)
+    )(dlogits, normed, loss, input_grad, gain_grad)
     return loss.reshape(1), input_grad, head_grad, gain_grad.reshape(depth)
 
 

time: 89.7 us -> 81.7 us (0.911)
  local copies, waits for them, and re-layouts: 3.2 us -> 0 us
  Pallas kernels: 83.5 us -> 80.8 us
  between operations: 2.49 us -> 0.64 us
    unnamed x7 -> x0, local copies, waits for them, and re-layouts: 3.2 us -> none
    pallas_call x1, Pallas kernels: 16.3 us -> 13.4 us  [per_device(): pl.pallas_call(head_grad_kernel, grid=(depth // wide,), out_shape=(jax.Sh...]
where the time goes in v2:
time: 81.7 us; the launch traced here: 81.4 us
  Pallas kernels  80.8 us (99%)
    pallas_call x1, Pallas kernels, per_device(): pl.pallas_call(functools.partial(head_kernel, n), out_shape=(jax.ShapeDty...  67.4 us
    pallas_call x1, Pallas kernels, per_device(): pl.pallas_call(head_grad_kernel, grid=(depth // wide,), out_shape=(jax.Sh...  13.4 us

profile of v2, /device:TPU:0, one launch (start us, length us, event | category | flops | bytes accessed | tf_op | source)
XLA Modules:
  0.0 81.4 jit_solution(2503865784276659572)
XLA Ops:
  0.6 67.4 %shard_map.84 = (f32[1,1]{1,0:T(1,128)}, bf16[8,8192]{1,0:T(8,128)(2,1)}, f32[2,1,4096]{2,1,0:T(1,128)}, bf16[1500,128]{1,0:T(8,128)(2,1)}, bf16[2,128,4096]{2,1,0:T(8,128)(2,1)}) custom-call(bf16[8,8192]{1,0:T(8,128)(2,1)} %resid_ref.1, f32[2,1,4096]{2,1,0:T(1,128)} %bitcast.6, bf16[1500,8192]{1,0:T(8,128)(2,1)} %head_ref.1, bf16[1500,128]{1,0:T(8,128)(2,1)} %bitcast.5, ...), custom_call_target="tpu_custom_call" | custom-call | flops 6291456000 | bytes 24576000 | tf_op jit(solution)/shard_map/pallas_call | solution.py:475
  68.0 13.4 %shard_map.85 = (bf16[1500,8192]{1,0:T(8,128)(2,1)}, f32[1,1]{1,0:T(1,128)}, bf16[8,8192]{1,0:T(8,128)(2,1)}, f32[2,1,4096]{2,1,0:T(1,128)}) custom-call(bf16[1500,128]{1,0:T(8,128)(2,1)} %get-tuple-element.13.dlogits_ref, bf16[2,128,4096]{2,1,0:T(8,128)(2,1)} %get-tuple-element.14.normed_ref, f32[1,1]{1,0:T(1,128)} %get-tuple-element.15.loss_in, ...), custom_call_target="tpu_custom_call" | custom-call | flops 3145728000 | bytes 24576000 | tf_op jit(solution)/shard_map/pallas_call | solution.py:546
